TPU v7x, 32 devices: a whole 2x2x4 slice. The times are simulated.
32 devices in a mesh: dp: 8 (over y, x, core), tensor: 4 (over z).
Axes of the slice: x: 2, y: 2, z: 4, core: 2. Of those that a mesh axis runs over, the one named last changes fastest.
Arguments:
- output_gradient: bfloat16 [2048, 8192], P('dp', 'tensor'), may hold values from -96 to 96
- hidden: bfloat16 [2048, 28672], P('dp', 'tensor'), may hold values from -3 to 3
- adapter_down: bfloat16 [16, 16, 28672], P('dp', None, 'tensor'), may hold values from -0.03125 to 0.03125
- adapter_up: bfloat16 [16, 16, 8192], P('dp', None, 'tensor'), may hold values from -0.0625 to 0.0625
- counts: int32 [16], replicated, may hold values from 32 to 288, as said below
- offsets: int32 [16], replicated, may hold values from 0 to 2016, as said below
- adapter_slot: int32 [16], replicated, may hold values from 0 to 15, as said below
Outputs:
- adapter_hidden_gradient: bfloat16 [2048, 28672], P('dp', 'tensor')
- adapter_down_gradient: float32 [16, 16, 28672], P('dp', None, 'tensor')
- adapter_up_gradient: float32 [16, 16, 8192], P('dp', None, 'tensor')
Inputs may be any that keep to these rules, and one draw needn't show every extreme that they name: counts sum to 2048; the last adapter has exactly 32 tokens; exactly one adapter has 288 tokens, every other fewer. Tokens are grouped by adapter in increasing order: offsets[a] is the sum of counts of the adapters before a. `adapter_slot`: every slot holds exactly one adapter; slot k lies on dp index k // 2, and any 16 // 2 adapters in a row lie on distinct dp indices.
All inputs are finite; a program needn't handle non-finite values.
Results may differ from a plain program's by a relative error of at most 0.0075.
Values may be sent and summed in bfloat16 or wider, within the bound.
A program may use at most 64 MiB of HBM per device.

v0:
```python
import jax
import jax.numpy as jnp
from jax import lax
from jax.sharding import PartitionSpec as P

adapter_factor = 2.0


def selected_rows(value_entries, shard_portion, member_rows):
    shard_count = shard_portion.shape[0]
    adapter_rank = shard_portion.shape[1]
    flattened_rows = shard_portion.reshape(shard_count * adapter_rank, shard_portion.shape[2])
    rank_scores = lax.dot_general(
        value_entries, flattened_rows, (((1,), (1,)), ((), ())), preferred_element_type=jnp.float32
    )
    selected_entries = member_rows.astype(jnp.float32)
    return jnp.sum(
        rank_scores.reshape(value_entries.shape[0], shard_count, adapter_rank)
        * selected_entries[:, :, None],
        axis=1,
    )


def on_device(output_gradient, hidden, adapter_down, adapter_up, counts, offsets, adapter_slot):
    total_rows = output_gradient.shape[0]
    slots_per_worker = adapter_down.shape[0]
    adapter_rank = adapter_down.shape[1]
    hidden_size_count = hidden.shape[1]
    dp_count = lax.axis_size("dp")
    adapter_list = slots_per_worker * dp_count
    first_token = lax.axis_index("dp") * total_rows
    positions = first_token + lax.broadcasted_iota(jnp.int32, (total_rows, 1), 0)
    inside = (positions >= offsets[None, :]) & (positions < (offsets + counts)[None, :])
    slot_of_row = jnp.sum(jnp.where(inside, adapter_slot[None, :], 0), axis=1)
    columns = lax.broadcasted_iota(jnp.int32, (1, adapter_list), 1)
    member_rows = (slot_of_row[:, None] == columns).astype(jnp.bfloat16)
    up_portion = selected_rows(
        output_gradient, lax.all_gather(adapter_up, "dp", axis=0, tiled=True), member_rows
    )
    up_incoming = lax.psum(up_portion, "tensor").astype(jnp.bfloat16)
    broadcast_up = member_rows[:, :, None] * up_incoming[:, None, :]
    shard_portion = lax.all_gather(adapter_down, "dp", axis=0, tiled=True)
    shard_count = shard_portion.shape[0]
    flattened_rows = shard_portion.reshape(shard_count * adapter_rank, hidden_size_count)
    down_partial = selected_rows(hidden, shard_portion, member_rows)
    broadcast_portion = broadcast_up
    broadcast_portion = broadcast_portion.reshape(total_rows, shard_count * adapter_rank)
    gradient_running = jnp.dot(
        broadcast_portion, flattened_rows, preferred_element_type=jnp.float32
    )
    down_partial, gradient_running = (down_partial, gradient_running)
    down_incoming = lax.psum(down_partial, "tensor").astype(jnp.bfloat16)
    adapter_hidden_gradient = (adapter_factor * gradient_running).astype(jnp.bfloat16)
    broadcast_down = member_rows[:, :, None] * down_incoming[:, None, :]

    def slot_term(spread, value_entries, shard_count):
        broadcast_portion = spread
        broadcast_portion = broadcast_portion.reshape(total_rows, shard_count * adapter_rank)
        matrix_product = lax.dot_general(
            broadcast_portion,
            value_entries,
            (((0,), (0,)), ((), ())),
            preferred_element_type=jnp.float32,
        )
        return matrix_product.reshape(shard_count, adapter_rank, value_entries.shape[1])

    joint_summed = lax.psum_scatter(
        jnp.concatenate(
            [
                slot_term(broadcast_up, hidden, slots_per_worker * lax.axis_size("dp")),
                slot_term(broadcast_down, output_gradient, slots_per_worker * lax.axis_size("dp")),
            ],
            axis=2,
        ).astype(jnp.bfloat16),
        "dp",
        scatter_dimension=0,
        tiled=True,
    ).astype(jnp.float32)
    down_reduced = joint_summed[:, :, :hidden_size_count]
    up_reduced = joint_summed[:, :, hidden_size_count:]
    slot_grid = adapter_slot[:, None] == columns
    total_slots = jnp.sum(jnp.where(slot_grid, counts[:, None], 0), axis=0)
    scale_entries = adapter_factor / total_slots.astype(jnp.float32)
    owner_scale = lax.dynamic_slice_in_dim(
        scale_entries, lax.axis_index("dp") * slots_per_worker, slots_per_worker, 0
    )
    adapter_down_gradient = down_reduced * owner_scale[:, None, None]
    adapter_up_gradient = up_reduced * owner_scale[:, None, None]
    return (adapter_hidden_gradient, adapter_down_gradient, adapter_up_gradient)


def solution(mesh):
    placed = (
        P("dp", "tensor"),
        P("dp", "tensor"),
        P("dp", None, "tensor"),
        P("dp", None, "tensor"),
        P(),
        P(),
        P(),
    )
    return jax.shard_map(
        on_device,
        mesh=mesh,
        in_specs=placed,
        out_specs=(P("dp", "tensor"), P("dp", None, "tensor"), P("dp", None, "tensor")),
        check_vma=False,
    )
```

profile of v0, /device:TPU:0, one launch (start us, length us, event | category | flops | bytes accessed | tf_op | source)
XLA Modules:
  0.0 162.8 jit_solution(15555558559586265905)
XLA Ops:
  7.2 0.0 copy-start
  7.2 0.0 all-gather.3.cloned.1.call-start
  7.2 0.7 all-gather.3.cloned.1.call-update
  7.9 0.0 all-gather.5.cloned.1.call-start
  8.0 0.7 all-gather.5.cloned.1.call-update
  8.7 0.0 reduce-scatter.2.cloned.1.call-start
  8.7 0.7 add.25
  9.4 0.8 select_reduce_fusion
  10.2 26.0 %all-gather.3.cloned.1.call-done = bf16[16,16,2048]{2,1,0:T(8,128)(2,1)} async-done(((bf16[2,16,2048]{2,1,0:T(8,128)(2,1)}), bf16[16,16,2048]{2,1,0:T(8,128)(2,1)}) %all-gather.3.cloned.1.call-update) | async-done | bytes 1048592 | tf_op jit(solution)/shard_map/all_gather | solution.py:38
  36.1 0.0 copy-done
  36.1 1.7 %fusion.11 = f32[256,16]{0,1:T(8,128)S(1)} fusion(bf16[16,16,2048]{2,1,0:T(8,128)(2,1)} %all-gather.3.cloned.1.call-done, bf16[256,2048]{1,0:T(8,128)(2,1)S(1)} %copy-done, f32[256,16]{0,1:T(8,128)S(1)} %get-tuple-element.6), kind=kOutput, calls=%fused_computation.12 | convolution fusion | flops 268562432 | bytes 2129920 | tf_op jit(solution)/shard_map/dot_general | solution.py:13
  37.8 34.7 %all-gather.5.cloned.1.call-done = bf16[16,16,7168]{2,1,0:T(8,128)(2,1)} async-done(((bf16[2,16,7168]{2,1,0:T(8,128)(2,1)}), bf16[16,16,7168]{2,1,0:T(8,128)(2,1)}) %all-gather.5.cloned.1.call-update) | async-done | bytes 3670032 | tf_op jit(solution)/shard_map/all_gather | solution.py:42
  72.6 4.3 %fusion.8 = f32[256,16]{0,1:T(8,128)S(1)} fusion(bf16[16,16,7168]{2,1,0:T(8,128)(2,1)} %all-gather.5.cloned.1.call-done, bf16[256,7168]{1,0:T(8,128)(2,1)} %param.8, f32[256,16]{0,1:T(8,128)S(1)} %get-tuple-element.6), kind=kOutput, calls=%fused_computation.11 | convolution fusion | flops 939651072 | bytes 7372800 | tf_op jit(solution)/shard_map/dot_general | solution.py:13
  76.9 19.0 %all-reduce = (bf16[256,16]{0,1:T(8,128)(2,1)S(1)}, bf16[256,16]{0,1:T(8,128)(2,1)S(1)}) all-reduce(f32[256,16]{0,1:T(8,128)S(1)} %fusion.11, f32[256,16]{0,1:T(8,128)S(1)} %fusion.8), channel_id=1, replica_groups=mesh['dp'=8,'tensor'=4] {'tensor'}, use_global_device_ids=true, to_apply=%region_2.3 | all-reduce | flops 8192 | bytes 49152 | tf_op jit(solution)/shard_map/psum | solution.py:40
  95.9 0.4 convolution_convert_fusion.1
  96.3 3.2 %convolution_convert_fusion = bf16[16,16,7168]{2,1,0:T(8,128)(2,1)S(1)} fusion(bf16[256,7168]{1,0:T(8,128)(2,1)} %param.8, bf16[256,16]{0,1:T(8,128)(2,1)S(1)} %get-tuple-element.3, bf16[256,16]{0,1:T(8,128)(2,1)S(1)} %get-tuple-element.5), kind=kOutput, calls=%fused_computation.3 | convolution fusion | flops 941424640 | bytes 7356416 | tf_op jit(solution)/shard_map/dot_general | solution.py:59
  99.5 2.4 %pad_maximum_fusion = bf16[16,16,9216]{2,1,0:T(8,128)(2,1)} fusion(bf16[16,16,2048]{2,1,0:T(8,128)(2,1)S(1)} %convolution_convert_fusion.1, bf16[16,16,7168]{2,1,0:T(8,128)(2,1)S(1)} %convolution_convert_fusion), kind=kLoop, calls=%fused_computation.4 | loop fusion | flops 9437184 | bytes 9437184 | tf_op jit(solution)/shard_map/concatenate | solution.py:68
  101.9 0.0 copy-start.1
  101.9 0.0 copy-start.2
  101.9 0.0 reduce-scatter.2.cloned.1.call-update
  102.0 0.6 copy-done.1
  102.6 0.0 copy-done.2
  102.6 0.1 select_reduce_fusion.1
  102.7 0.1 dynamic_slice.3
  102.8 5.1 %fusion.1 = bf16[256,7168]{1,0:T(8,128)(2,1)} fusion(bf16[16,16,7168]{2,1,0:T(8,128)(2,1)} %all-gather.5.cloned.1.call-done, bf16[256,16]{0,1:T(8,128)(2,1)S(1)} %get-tuple-element.3, bf16[256,16]{0,1:T(8,128)(2,1)S(1)} %get-tuple-element.5), kind=kOutput, calls=%fused_computation.2 | convolution fusion | flops 943259648 | bytes 7356416 | tf_op jit(solution)/shard_map/dot_general | solution.py:48
  107.8 45.4 %reduce-scatter.2.cloned.1.call-done = bf16[2,16,9216]{2,1,0:T(8,128)(2,1)} async-done(((bf16[16,16,9216]{2,1,0:T(8,128)(2,1)}), bf16[2,16,9216]{2,1,0:T(8,128)(2,1)}) %reduce-scatter.2.cloned.1.call-update) | async-done | bytes 589840 | tf_op jit(solution)/shard_map/reduce_scatter | solution.py:67
  153.3 1.1 convert_element_type.39
  154.4 0.8 slice_multiply_fusion.1
  155.2 1.0 slice_multiply_fusion
  (3 shorter events, 0.0 us)
Async XLA Ops:
  7.2 29.0 %copy-start = (bf16[256,2048]{1,0:T(8,128)(2,1)S(1)}, bf16[256,2048]{1,0:T(8,128)(2,1)}, u32[]{:S(2)}) copy-start(bf16[256,2048]{1,0:T(8,128)(2,1)} %param.7) | copy-start | bytes 3145732
  7.2 28.9 %all-gather.3.cloned.1.call-start = ((), (), s32[]{:S(2)}) async-start(), calls=%async_computation.1 | async-start | bytes 1179648 | tf_op jit(solution)/shard_map/all_gather | solution.py:38
  7.9 64.6 %all-gather.5.cloned.1.call-start = ((), (), s32[]{:S(2)}) async-start(), calls=%async_computation.2 | async-start | bytes 4128768 | tf_op jit(solution)/shard_map/all_gather | solution.py:42
  8.7 144.6 %reduce-scatter.2.cloned.1.call-start = ((), (), s32[]{:S(2)}) async-start(), calls=%async_computation.3 | async-start | bytes 5308416 | tf_op jit(solution)/shard_map/reduce_scatter | solution.py:67
  101.9 0.7 copy-start.1
  101.9 0.7 copy-start.2
Sparse Core Ops, SparseCore 0:
  9.9 26.1 all-gather.2
  38.0 34.4 all-gather.4
  102.1 51.1 reduce-scatter.1
where the time goes:
time: 163 us
  waiting for transfers between devices  107 us (66%)
  blocking collectives  19 us (12%)
  matrix products  14.7 us (9%)
  between operations  13.8 us (8%)
  other arithmetic  6.95 us (4%)
    reduce_scatter x1, waiting for transfers between devices, on_device(): lax.psum_scatter(jnp.concatenate([slot_term(broadcast_up, hidden, slots_p...  45.4 us
    all_gather x1, waiting for transfers between devices, on_device(): shard_portion = lax.all_gather(adapter_down, 'dp', axis=0, tiled=True)  34.7 us
    all_gather x1, waiting for transfers between devices, on_device(): lax.all_gather(adapter_up, 'dp', axis=0, tiled=True)  26 us
    psum x1, blocking collectives, on_device(): up_incoming = lax.psum(up_portion, 'tensor').astype(jnp.bfloat16)  19 us
    dot_general x2, matrix products, selected_rows(): lax.dot_general(value_entries, flattened_rows, (((1,), (1,)), ((), ())),...  6 us
    dot_general x1, matrix products, on_device(): jnp.dot(broadcast_portion, flattened_rows, preferred_element_type=jnp.flo...  5.07 us
    dot_general x2, matrix products, slot_term(): lax.dot_general(broadcast_portion, value_entries, (((0,), (0,)), ((), ())...  3.6 us
  transfers between devices with their start and end apart: 3, of which 3 were waited for; matrix products, arithmetic and copies ran while one was open for 5% of the time, Pallas kernels for 0%

commit v1 on v0

v1 whole, which is shorter than its diff:
```python
import functools
import math

import jax
import jax.numpy as jnp
from jax import lax
from jax.experimental import pallas as pl
from jax.experimental.pallas import tpu as pltpu
from jax.sharding import PartitionSpec as P

adapter_factor = 2.0
MESH = pl.DeviceIdType.MESH


def chip_grid(dp_count):
    chips = dp_count // 2
    second = max(d for d in range(1, math.isqrt(chips) + 1) if chips % d == 0)
    return chips // second, second


def kernel(
    dp_count, tensor_count, sends,
    counts, offsets, slots, og, hid, adn, aup,
    out_h, out_d, out_u,
    gath_d, gath_u, z_up, z_dn,
    sib_d, sib_u, got_d, got_u, sum_d, sum_u,
    one_d0, one_d1, one_u0, one_u1, two_d0, two_d1, two_u0, two_u1,
    send_sem, gath_sem, z_sem, sib_sem, one_sem0, one_sem1, two_sem0, two_sem1,
):
    size_a, size_b = chip_grid(dp_count)
    chips = size_a * size_b
    tokens = og.shape[0]
    per_owner, rank = adn.shape[0], adn.shape[1]
    me = lax.axis_index("dp")
    me_t = lax.axis_index("tensor")
    core = me % 2
    chip = me // 2
    at_a, at_b = chip // size_b, chip % size_b
    sibling = chip * 2 + (1 - core)

    def chip_of(half, first, second):
        return first * size_b + second if half == 0 else second * size_b + first

    def axes(half):
        if half == 0:
            return at_a, size_a, at_b, size_b
        return at_b, size_b, at_a, size_a

    started = []

    def push(src, dst, recv, **device):
        copy = pltpu.make_async_remote_copy(
            src_ref=src, dst_ref=dst, send_sem=send_sem.at[len(started)], recv_sem=recv,
            device_id=device, device_id_type=MESH,
        )
        copy.start()
        started.append(copy)

    def arrived(dst, recv):
        pltpu.make_async_remote_copy(
            src_ref=dst, dst_ref=dst, send_sem=send_sem.at[0], recv_sem=recv,
            device_id={"dp": sibling}, device_id_type=MESH,
        ).wait_recv()

    barrier = pltpu.get_barrier_semaphore()
    partners = [{"dp": sibling}]
    for off in range(1, size_a):
        partners.append({"dp": (((at_a + off) % size_a) * size_b + at_b) * 2 + core})
    for off in range(1, size_b):
        partners.append({"dp": (at_a * size_b + (at_b + off) % size_b) * 2 + core})
    for off in range(1, tensor_count):
        partners.append({"tensor": (me_t + off) % tensor_count})
    for partner in partners:
        pl.semaphore_signal(barrier, inc=1, device_id=partner, device_id_type=MESH)
    pl.semaphore_wait(barrier, len(partners))

    def gather_own(which, own, gath):
        for half in range(per_owner):
            first, n_first, second, n_second = axes(half)
            recv = gath_sem.at[which, me, half]
            for off in range(1, n_first):
                to = chip_of(half, (first + off) % n_first, second) * 2 + core
                push(own.at[half], gath.at[me, half], recv, dp=to)
            for off in range(1, n_second):
                to = chip_of(half, first, (second + off) % n_second) * 2 + core
                push(own.at[half], gath.at[me, half], recv, dp=to)
            push(own.at[half], gath.at[me, half], recv, dp=sibling)

    def gather_first(which, gath):
        for half in range(per_owner):
            first, n_first, second, n_second = axes(half)
            for off in range(1, n_first):
                origin = chip_of(half, (first + off) % n_first, second) * 2 + core
                block, recv = gath.at[origin, half], gath_sem.at[which, origin, half]
                arrived(block, recv)
                for off2 in range(1, n_second):
                    to = chip_of(half, first, (second + off2) % n_second) * 2 + core
                    push(block, block, recv, dp=to)
                push(block, block, recv, dp=sibling)

    def gather_second(which, gath):
        for near in (True, False):
            for half in range(per_owner):
                first, n_first, second, n_second = axes(half)
                for off2 in range(1, n_second):
                    for off in range(0, 1) if near else range(1, n_first):
                        origin = chip_of(
                            half, (first + off) % n_first, (second + off2) % n_second
                        ) * 2 + core
                        block, recv = gath.at[origin, half], gath_sem.at[which, origin, half]
                        arrived(block, recv)
                        push(block, block, recv, dp=sibling)

    def gather_sibling(which, gath):
        for other in range(chips):
            for half in range(per_owner):
                origin = other * 2 + (1 - core)
                arrived(gath.at[origin, half], gath_sem.at[which, origin, half])

    gather_own(0, aup, gath_u)
    gather_own(1, adn, gath_d)
    gath_u[pl.ds(me, 1)] = aup[...][None]
    gath_d[pl.ds(me, 1)] = adn[...][None]

    position = me * tokens + lax.broadcasted_iota(jnp.int32, (1, tokens), 1)
    slot_of = jnp.zeros((1, tokens), jnp.int32)
    for adapter in range(counts.shape[0]):
        low = offsets[adapter]
        inside = (position >= low) & (position < low + counts[adapter])
        slot_of = slot_of + jnp.where(inside, slots[adapter], 0)

    def tile_of(width):
        return math.gcd(width, 512)

    def partial_signal(values, gath):
        width = values.shape[1]
        tile = tile_of(width)
        rows = dp_count * per_owner * rank

        def step(at, total):
            cols = pl.ds(pl.multiple_of(at * tile, tile), tile)
            maps = gath[:, :, :, cols].reshape(rows, tile)
            return total + lax.dot_general(
                maps, values[:, cols], (((1,), (1,)), ((), ())),
                preferred_element_type=jnp.float32,
            )

        scores = lax.fori_loop(
            0, width // tile, step, jnp.zeros((rows, tokens), jnp.float32)
        ).reshape(dp_count * per_owner, rank, tokens)
        total = jnp.zeros((rank, tokens), jnp.float32)
        for slot in range(dp_count * per_owner):
            total = total + jnp.where(slot_of == slot, scores[slot], 0.0)
        return total

    def share(which, buffer, value):
        buffer[pl.ds(me_t, 1)] = value[None]
        for off in range(1, tensor_count):
            push(
                buffer.at[me_t], buffer.at[me_t], z_sem.at[which, me_t],
                tensor=(me_t + off) % tensor_count,
            )

    def shared(which, buffer):
        for off in range(1, tensor_count):
            origin = (me_t + off) % tensor_count
            arrived(buffer.at[origin], z_sem.at[which, origin])
        total = buffer[0]
        for origin in range(1, tensor_count):
            total = total + buffer[origin]
        return total.astype(jnp.bfloat16).astype(jnp.float32)

    def spread(signal, numbers):
        return jnp.concatenate(
            [jnp.where(slot_of == number, signal, 0.0) for number in numbers], axis=0
        )

    def numbers_of(which_core):
        return [
            (other * 2 + which_core) * per_owner + half
            for other in range(chips)
            for half in range(per_owner)
        ]

    def sums_sibling(which, signal, values, sib, got):
        rows = spread(signal, numbers_of(1 - core)).astype(jnp.bfloat16)
        width = values.shape[1]
        tile = tile_of(width)

        def step(at, _):
            cols = pl.ds(pl.multiple_of(at * tile, tile), tile)
            term = jnp.dot(rows, values[:, cols], preferred_element_type=jnp.float32)
            sib[:, :, :, cols] = term.astype(jnp.bfloat16).reshape(chips, per_owner, rank, tile)
            return 0

        lax.fori_loop(0, width // tile, step, 0)
        push(sib, got, sib_sem.at[which], dp=sibling)

    def sums_first(which, signal, values, got, total, one):
        rows = spread(signal, numbers_of(core)).astype(jnp.bfloat16)
        width = values.shape[1]
        tile = tile_of(width)
        arrived(got, sib_sem.at[which])

        def step(at, _):
            cols = pl.ds(pl.multiple_of(at * tile, tile), tile)
            term = jnp.dot(rows, values[:, cols], preferred_element_type=jnp.float32)
            term = term.reshape(chips, per_owner, rank, tile)
            term = term + got[:, :, :, cols].astype(jnp.float32)
            total[:, :, :, cols] = term.astype(jnp.bfloat16)
            return 0

        lax.fori_loop(0, width // tile, step, 0)
        sems = (one_sem0, one_sem1)
        for far in (True, False):
            for half in range(per_owner):
                first, n_first, second, n_second = axes(half)
                for off in range(1, n_first):
                    peer = (first + off) % n_first
                    to = chip_of(half, peer, second) * 2 + core
                    for off2 in range(1, n_second) if far else range(0, 1):
                        owner_second = (second + off2) % n_second
                        push(
                            total.at[chip_of(half, peer, owner_second), half],
                            one[half].at[first, owner_second],
                            sems[half].at[which, first, owner_second],
                            dp=to,
                        )

    def sums_second(which, total, one, two):
        sems, sems2 = (one_sem0, one_sem1), (two_sem0, two_sem1)
        for half in range(per_owner):
            first, n_first, second, n_second = axes(half)
            for off2 in range(1, n_second):
                owner_second = (second + off2) % n_second
                owner = chip_of(half, first, owner_second)
                value = total[owner, half].astype(jnp.float32)
                for off in range(1, n_first):
                    peer = (first + off) % n_first
                    arrived(
                        one[half].at[peer, owner_second],
                        sems[half].at[which, peer, owner_second],
                    )
                    value = value + one[half][peer, owner_second].astype(jnp.float32)
                total[pl.ds(owner, 1), half] = value.astype(jnp.bfloat16)[None]
                push(
                    total.at[owner, half], two[half].at[second],
                    sems2[half].at[which, second], dp=owner * 2 + core,
                )

    def sums_last(which, total, one, two, out):
        sems, sems2 = (one_sem0, one_sem1), (two_sem0, two_sem1)
        for half in range(per_owner):
            first, n_first, second, n_second = axes(half)
            value = total[chip, half].astype(jnp.float32)
            for off in range(1, n_first):
                peer = (first + off) % n_first
                arrived(one[half].at[peer, second], sems[half].at[which, peer, second])
                value = value + one[half][peer, second].astype(jnp.float32)
            for off2 in range(1, n_second):
                peer = (second + off2) % n_second
                arrived(two[half].at[peer], sems2[half].at[which, peer])
                value = value + two[half][peer].astype(jnp.float32)
            number = me * per_owner + half
            held = jnp.zeros((1, 1), jnp.int32)
            for adapter in range(counts.shape[0]):
                mine = jnp.full((1, 1), slots[adapter], jnp.int32) == number
                held = held + jnp.where(mine, counts[adapter], 0)
            out[half] = value * (adapter_factor / held.astype(jnp.float32))

    one_d, one_u = (one_d0, one_d1), (one_u0, one_u1)
    two_d, two_u = (two_d0, two_d1), (two_u0, two_u1)

    gather_first(0, gath_u)
    gather_second(0, gath_u)
    gather_sibling(0, gath_u)
    share(0, z_up, partial_signal(og, gath_u))
    gather_first(1, gath_d)
    up_signal = shared(0, z_up)
    sums_sibling(0, up_signal, hid, sib_d, got_d)
    gather_second(1, gath_d)
    sums_first(0, up_signal, hid, got_d, sum_d, one_d)
    gather_sibling(1, gath_d)
    share(1, z_dn, partial_signal(hid, gath_d))

    all_rows = dp_count * per_owner * rank
    tokens_by_row = spread(up_signal, range(dp_count * per_owner)).T.astype(jnp.bfloat16)
    tile = tile_of(hid.shape[1])

    def hidden_step(at, _):
        cols = pl.ds(pl.multiple_of(at * tile, tile), tile)
        maps = gath_d[:, :, :, cols].reshape(all_rows, tile)
        term = jnp.dot(tokens_by_row, maps, preferred_element_type=jnp.float32)
        out_h[:, cols] = (adapter_factor * term).astype(out_h.dtype)
        return 0

    lax.fori_loop(0, hid.shape[1] // tile, hidden_step, 0)

    down_signal = shared(1, z_dn)
    sums_sibling(1, down_signal, og, sib_u, got_u)
    sums_second(0, sum_d, one_d, two_d)
    sums_first(1, down_signal, og, got_u, sum_u, one_u)
    sums_second(1, sum_u, one_u, two_u)
    sums_last(0, sum_d, one_d, two_d, out_d)
    sums_last(1, sum_u, one_u, two_u, out_u)
    for copy in started:
        copy.wait_send()
    assert len(started) == sends, (len(started), sends)


def send_count(dp_count, tensor_count, per_owner):
    size_a, size_b = chip_grid(dp_count)
    total = 2 * (tensor_count - 1) + 2
    for half in range(per_owner):
        n_first, n_second = (size_a, size_b) if half == 0 else (size_b, size_a)
        own = n_first + n_second - 1
        relayed = (n_first - 1) * n_second + (n_second - 1) * n_first
        back = (n_first - 1) * n_second + (n_second - 1)
        total += 2 * (own + relayed + back)
    return total


def on_device(output_gradient, hidden, adapter_down, adapter_up, counts, offsets, adapter_slot):
    dp_count, tensor_count = lax.axis_size("dp"), lax.axis_size("tensor")
    size_a, size_b = chip_grid(dp_count)
    chips = size_a * size_b
    per_owner, rank, wide = adapter_down.shape
    narrow = adapter_up.shape[2]
    tokens = hidden.shape[0]
    sends = send_count(dp_count, tensor_count, per_owner)
    bf16, f32 = jnp.bfloat16, jnp.float32
    dma = pltpu.SemaphoreType.DMA
    vmem = pl.BlockSpec(memory_space=pltpu.VMEM)
    smem = pl.BlockSpec(memory_space=pltpu.SMEM)
    scratch = [
        pltpu.VMEM((dp_count, per_owner, rank, wide), bf16),
        pltpu.VMEM((dp_count, per_owner, rank, narrow), bf16),
        pltpu.VMEM((tensor_count, rank, tokens), f32),
        pltpu.VMEM((tensor_count, rank, tokens), f32),
    ]
    for _ in range(3):
        scratch.append(pltpu.VMEM((chips, per_owner, rank, wide), bf16))
        scratch.append(pltpu.VMEM((chips, per_owner, rank, narrow), bf16))
    for width in (wide, narrow):
        scratch.append(pltpu.VMEM((size_a, size_b, rank, width), bf16))
        scratch.append(pltpu.VMEM((size_b, size_a, rank, width), bf16))
    for width in (wide, narrow):
        scratch.append(pltpu.VMEM((size_b, rank, width), bf16))
        scratch.append(pltpu.VMEM((size_a, rank, width), bf16))
    scratch += [
        dma((sends,)),
        dma((2, dp_count, per_owner)),
        dma((2, tensor_count)),
        dma((2,)),
        dma((2, size_a, size_b)),
        dma((2, size_b, size_a)),
        dma((2, size_b)),
        dma((2, size_a)),
    ]
    rows = dp_count * per_owner * rank
    return pl.pallas_call(
        functools.partial(kernel, dp_count, tensor_count, sends),
        out_shape=(
            jax.ShapeDtypeStruct((tokens, wide), bf16),
            jax.ShapeDtypeStruct((per_owner, rank, wide), f32),
            jax.ShapeDtypeStruct((per_owner, rank, narrow), f32),
        ),
        in_specs=[smem] * 3 + [vmem] * 4,
        out_specs=(vmem, vmem, vmem),
        scratch_shapes=scratch,
        compiler_params=pltpu.CompilerParams(
            collective_id=0, has_side_effects=True, vmem_limit_bytes=56 * 2**20
        ),
        cost_estimate=pl.CostEstimate(
            flops=2 * rows * tokens * (3 * wide + 2 * narrow),
            bytes_accessed=2 * tokens * (2 * wide + narrow),
            transcendentals=0,
        ),
    )(counts, offsets, adapter_slot, output_gradient, hidden, adapter_down, adapter_up)


def solution(mesh):
    placed = (
        P("dp", "tensor"),
        P("dp", "tensor"),
        P("dp", None, "tensor"),
        P("dp", None, "tensor"),
        P(),
        P(),
        P(),
    )
    return jax.shard_map(
        on_device,
        mesh=mesh,
        in_specs=placed,
        out_specs=(P("dp", "tensor"), P("dp", None, "tensor"), P("dp", None, "tensor")),
        check_vma=False,
    )
```

time: 163 us -> 69 us (0.42)
  waiting for transfers between devices: 107 us -> 0 us
  Pallas kernels: 0 us -> 62.4 us
  blocking collectives: 19 us -> 0 us
  matrix products: 14.7 us -> 0 us
  between operations: 13.8 us -> 0.66 us
  other arithmetic: 6.95 us -> 0 us
  local copies, waits for them, and re-layouts: 0.73 us -> 5.84 us
    pallas_call x0 -> x1, Pallas kernels: none -> 62.4 us  [on_device(): pl.pallas_call(functools.partial(kernel, dp_count, tensor_count, sends),...]
    all_gather x2 -> x0, waiting for transfers between devices: 60.7 us -> none  [the longest x1 34.7 us: on_device(): shard_portion = lax.all_gather(adapter_down, 'dp', axis=0, tiled=True)]
    reduce_scatter x1 -> x0, waiting for transfers between devices: 45.4 us -> none  [on_device(): lax.psum_scatter(jnp.concatenate([slot_term(broadcast_up, hidden, slots_p...]
    psum x1 -> x0, blocking collectives: 19 us -> none  [on_device(): up_incoming = lax.psum(up_portion, 'tensor').astype(jnp.bfloat16)]
    dot_general x5 -> x0, matrix products: 14.7 us -> none  [the longest x2 6 us: selected_rows(): lax.dot_general(value_entries, flattened_rows, (((1,), (1,)), ((), ())),...]
    unnamed x6 -> x7, local copies, waits for them, and re-layouts: 0.65 us -> 5.84 us
    concatenate x1 -> x0, other arithmetic: 2.43 us -> none  [on_device(): jnp.concatenate([slot_term(broadcast_up, hidden, slots_per_worker * lax.a...]
    mul x2 -> x0, other arithmetic: 1.84 us -> none  [the longest x1 1.05 us: on_device(): adapter_down_gradient = down_reduced * owner_scale[:, None, None]]
  transfers between devices with their start and end apart: 3 -> 0, of which waited for: 3 -> 0; matrix products, arithmetic and copies ran while one was open for 5% -> 0% of each run, Pallas kernels for 0% -> 0%
where the time goes in v1:
time: 69 us; the launch traced here: 68.9 us
  Pallas kernels  62.4 us (90%)
  local copies, waits for them, and re-layouts  5.84 us (8%)
    pallas_call x1, Pallas kernels, on_device(): pl.pallas_call(functools.partial(kernel, dp_count, tensor_count, sends),...  62.4 us
    unnamed x7, local copies, waits for them, and re-layouts  5.84 us

profile of v1, /device:TPU:0, one launch (start us, length us, event | category | flops | bytes accessed | tf_op | source)
XLA Modules:
  0.0 68.9 jit_solution(4435289459958572121)
XLA Ops:
  0.6 62.4 %shard_map.94 = (bf16[256,7168]{1,0:T(8,128)(2,1)}, f32[2,16,7168]{2,1,0:T(8,128)}, f32[2,16,2048]{2,1,0:T(8,128)}) custom-call(s32[16]{0:T(128)} %counts.1, s32[16]{0:T(128)} %offsets.1, s32[16]{0:T(128)} %slots.1, bf16[256,2048]{1,0:T(8,128)(2,1)} %og.1, bf16[256,7168]{1,0:T(8,128)(2,1)} %hid.1, bf16[2,16,7168]{2,1,0:T(8,128)(2,1)} %adn.1, ...), custom_call_target="tpu_custom_call" | custom-call | flops 3355443200 | bytes 8388608 | tf_op jit(solution)/shard_map/pallas_call | solution.py:361
  63.0 0.0 copy-start
  63.0 0.0 copy-start.1
  63.0 4.2 %copy.13 = bf16[256,7168]{1,0:T(8,128)(2,1)} copy(bf16[256,7168]{1,0:T(8,128)(2,1)} %get-tuple-element.6) | data formatting | bytes 7340032
  67.2 0.0 copy-done
  67.2 0.9 %copy.14 = f32[2,16,7168]{2,1,0:T(8,128)} copy(f32[2,16,7168]{2,1,0:T(8,128)S(1)} %copy-done) | data formatting | bytes 1835008
  68.2 0.0 copy-done.1
  68.2 0.7 %copy.15 = f32[2,16,2048]{2,1,0:T(8,128)} copy(f32[2,16,2048]{2,1,0:T(8,128)S(1)} %copy-done.1) | data formatting | bytes 524288
Async XLA Ops:
  63.0 4.2 %copy-start = (f32[2,16,7168]{2,1,0:T(8,128)S(1)}, f32[2,16,7168]{2,1,0:T(8,128)}, u32[]{:S(2)}) copy-start(f32[2,16,7168]{2,1,0:T(8,128)} %get-tuple-element.7) | copy-start | bytes 2752516
  63.0 5.1 %copy-start.1 = (f32[2,16,2048]{2,1,0:T(8,128)S(1)}, f32[2,16,2048]{2,1,0:T(8,128)}, u32[]{:S(2)}) copy-start(f32[2,16,2048]{2,1,0:T(8,128)} %get-tuple-element.8) | copy-start | bytes 786436

commit v2 on v1

--- a/solution.py
+++ b/solution.py
@@ -20,12 +20,12 @@
 
 def kernel(
     dp_count, tensor_count, sends,
-    counts, offsets, slots, og, hid, adn, aup,
+    counts, offsets, slots, og_in, hid_in, adn, aup,
     out_h, out_d, out_u,
-    gath_d, gath_u, z_up, z_dn,
+    og, hid, gath_d, gath_u, z_up, z_dn,
     sib_d, sib_u, got_d, got_u, sum_d, sum_u,
     one_d0, one_d1, one_u0, one_u1, two_d0, two_d1, two_u0, two_u1,
-    send_sem, gath_sem, z_sem, sib_sem, one_sem0, one_sem1, two_sem0, two_sem1,
+    load_sem, send_sem, gath_sem, z_sem, sib_sem, one_sem0, one_sem1, two_sem0, two_sem1,
 ):
     size_a, size_b = chip_grid(dp_count)
     chips = size_a * size_b
@@ -62,6 +62,15 @@
             device_id={"dp": sibling}, device_id_type=MESH,
         ).wait_recv()
 
+    loads = [
+        pltpu.make_async_copy(aup, gath_u.at[me], load_sem.at[0]),
+        pltpu.make_async_copy(og_in, og, load_sem.at[1]),
+        pltpu.make_async_copy(hid_in, hid, load_sem.at[2]),
+        pltpu.make_async_copy(adn, gath_d.at[me], load_sem.at[3]),
+    ]
+    for load in loads:
+        load.start()
+
     barrier = pltpu.get_barrier_semaphore()
     partners = [{"dp": sibling}]
     for off in range(1, size_a):
@@ -75,16 +84,18 @@
     pl.semaphore_wait(barrier, len(partners))
 
     def gather_own(which, own, gath):
+        for along_first in (True, False):
+            for half in range(per_owner):
+                first, n_first, second, n_second = axes(half)
+                recv = gath_sem.at[which, me, half]
+                for off in range(1, n_first if along_first else n_second):
+                    if along_first:
+                        to = chip_of(half, (first + off) % n_first, second) * 2 + core
+                    else:
+                        to = chip_of(half, first, (second + off) % n_second) * 2 + core
+                    push(own.at[half], gath.at[me, half], recv, dp=to)
         for half in range(per_owner):
-            first, n_first, second, n_second = axes(half)
-            recv = gath_sem.at[which, me, half]
-            for off in range(1, n_first):
-                to = chip_of(half, (first + off) % n_first, second) * 2 + core
-                push(own.at[half], gath.at[me, half], recv, dp=to)
-            for off in range(1, n_second):
-                to = chip_of(half, first, (second + off) % n_second) * 2 + core
-                push(own.at[half], gath.at[me, half], recv, dp=to)
-            push(own.at[half], gath.at[me, half], recv, dp=sibling)
+            push(own.at[half], gath.at[me, half], gath_sem.at[which, me, half], dp=sibling)
 
     def gather_first(which, gath):
         for half in range(per_owner):
@@ -118,10 +129,6 @@
                 arrived(gath.at[origin, half], gath_sem.at[which, origin, half])
 
     gather_own(0, aup, gath_u)
-    gather_own(1, adn, gath_d)
-    gath_u[pl.ds(me, 1)] = aup[...][None]
-    gath_d[pl.ds(me, 1)] = adn[...][None]
-
     position = me * tokens + lax.broadcasted_iota(jnp.int32, (1, tokens), 1)
     slot_of = jnp.zeros((1, tokens), jnp.int32)
     for adapter in range(counts.shape[0]):
@@ -272,15 +279,20 @@
     two_d, two_u = (two_d0, two_d1), (two_u0, two_u1)
 
     gather_first(0, gath_u)
+    gather_own(1, adn, gath_d)
     gather_second(0, gath_u)
     gather_sibling(0, gath_u)
+    loads[0].wait()
+    loads[1].wait()
     share(0, z_up, partial_signal(og, gath_u))
-    gather_first(1, gath_d)
+    loads[2].wait()
     up_signal = shared(0, z_up)
     sums_sibling(0, up_signal, hid, sib_d, got_d)
+    gather_first(1, gath_d)
+    sums_first(0, up_signal, hid, got_d, sum_d, one_d)
     gather_second(1, gath_d)
-    sums_first(0, up_signal, hid, got_d, sum_d, one_d)
     gather_sibling(1, gath_d)
+    loads[3].wait()
     share(1, z_dn, partial_signal(hid, gath_d))
 
     all_rows = dp_count * per_owner * rank
@@ -298,8 +310,8 @@
 
     down_signal = shared(1, z_dn)
     sums_sibling(1, down_signal, og, sib_u, got_u)
+    sums_first(1, down_signal, og, got_u, sum_u, one_u)
     sums_second(0, sum_d, one_d, two_d)
-    sums_first(1, down_signal, og, got_u, sum_u, one_u)
     sums_second(1, sum_u, one_u, two_u)
     sums_last(0, sum_d, one_d, two_d, out_d)
     sums_last(1, sum_u, one_u, two_u, out_u)
@@ -333,6 +345,8 @@
     vmem = pl.BlockSpec(memory_space=pltpu.VMEM)
     smem = pl.BlockSpec(memory_space=pltpu.SMEM)
     scratch = [
+        pltpu.VMEM((tokens, narrow), bf16),
+        pltpu.VMEM((tokens, wide), bf16),
         pltpu.VMEM((dp_count, per_owner, rank, wide), bf16),
         pltpu.VMEM((dp_count, per_owner, rank, narrow), bf16),
         pltpu.VMEM((tensor_count, rank, tokens), f32),
@@ -348,6 +362,7 @@
         scratch.append(pltpu.VMEM((size_b, rank, width), bf16))
         scratch.append(pltpu.VMEM((size_a, rank, width), bf16))
     scratch += [
+        dma((4,)),
         dma((sends,)),
         dma((2, dp_count, per_owner)),
         dma((2, tensor_count)),
@@ -361,15 +376,15 @@
     return pl.pallas_call(
         functools.partial(kernel, dp_count, tensor_count, sends),
         out_shape=(
-            jax.ShapeDtypeStruct((tokens, wide), bf16),
-            jax.ShapeDtypeStruct((per_owner, rank, wide), f32),
-            jax.ShapeDtypeStruct((per_owner, rank, narrow), f32),
+            pltpu.VMEM((tokens, wide), bf16),
+            pltpu.VMEM((per_owner, rank, wide), f32),
+            pltpu.VMEM((per_owner, rank, narrow), f32),
         ),
-        in_specs=[smem] * 3 + [vmem] * 4,
+        in_specs=[smem] * 3 + [pl.BlockSpec(memory_space=pl.ANY)] * 4,
         out_specs=(vmem, vmem, vmem),
         scratch_shapes=scratch,
         compiler_params=pltpu.CompilerParams(
-            collective_id=0, has_side_effects=True, vmem_limit_bytes=56 * 2**20
+            collective_id=0, has_side_effects=True, vmem_limit_bytes=48 * 2**20
         ),
         cost_estimate=pl.CostEstimate(
             flops=2 * rows * tokens * (3 * wide + 2 * narrow),

time: 69 us -> 62.7 us (0.909)
  Pallas kernels: 62.4 us -> 54.5 us
  local copies, waits for them, and re-layouts: 5.84 us -> 7.34 us
    pallas_call x1, Pallas kernels: 62.4 us -> 54.5 us  [on_device(): pl.pallas_call(functools.partial(kernel, dp_count, tensor_count, sends),...]
    unnamed x7 -> x13, local copies, waits for them, and re-layouts: 5.84 us -> 7.34 us
where the time goes in v2:
time: 62.7 us; the launch traced here: 62.5 us
  Pallas kernels  54.5 us (87%)
  local copies, waits for them, and re-layouts  7.34 us (12%)
  between operations  0.65 us (1%)
    pallas_call x1, Pallas kernels, on_device(): pl.pallas_call(functools.partial(kernel, dp_count, tensor_count, sends),...  54.5 us
    unnamed x13, local copies, waits for them, and re-layouts  7.34 us

profile of v2, /device:TPU:0, one launch (start us, length us, event | category | flops | bytes accessed | tf_op | source)
XLA Modules:
  0.0 62.5 jit_solution(14022487324879521807)
XLA Ops:
  0.6 0.0 copy-start
  0.6 1.0 %copy-done = bf16[2,16,7168]{2,1,0:T(8,128)(2,1)S(1)} copy-done((bf16[2,16,7168]{2,1,0:T(8,128)(2,1)S(1)}, bf16[2,16,7168]{2,1,0:T(8,128)(2,1)}, u32[]{:S(2)}) %copy-start) | copy-done | bytes 458776
  1.7 0.0 copy-start.1
  1.7 0.9 %copy-done.1 = bf16[2,16,2048]{2,1,0:T(8,128)(2,1)S(1)} copy-done((bf16[2,16,2048]{2,1,0:T(8,128)(2,1)S(1)}, bf16[2,16,2048]{2,1,0:T(8,128)(2,1)}, u32[]{:S(2)}) %copy-start.1) | copy-done | bytes 131096
  2.6 0.0 copy-start.2
  2.6 0.7 %copy-done.2 = s32[16]{0:T(128)S(1)} copy-done((s32[16]{0:T(128)S(1)}, s32[16]{0:T(128)}, u32[]{:S(2)}) %copy-start.2) | copy-done | bytes 88
  3.2 0.0 copy-start.3
  3.2 0.7 %copy-done.3 = s32[16]{0:T(128)S(1)} copy-done((s32[16]{0:T(128)S(1)}, s32[16]{0:T(128)}, u32[]{:S(2)}) %copy-start.3) | copy-done | bytes 88
  3.9 0.0 copy-start.4
  3.9 0.7 %copy-done.4 = s32[16]{0:T(128)S(1)} copy-done((s32[16]{0:T(128)S(1)}, s32[16]{0:T(128)}, u32[]{:S(2)}) %copy-start.4) | copy-done | bytes 88
  4.5 54.5 %shard_map.94 = (bf16[256,7168]{1,0:T(8,128)(2,1)S(1)}, f32[2,16,7168]{2,1,0:T(8,128)S(1)}, f32[2,16,2048]{2,1,0:T(8,128)S(1)}) custom-call(s32[16]{0:T(128)S(1)} %copy-done.2, s32[16]{0:T(128)S(1)} %copy-done.3, s32[16]{0:T(128)S(1)} %copy-done.4, bf16[256,2048]{1,0:T(8,128)(2,1)} %og_in.1, bf16[256,7168]{1,0:T(8,128)(2,1)} %hid_in.1, ...), custom_call_target="tpu_custom_call" | custom-call | flops 3355443200 | bytes 8388608 | tf_op jit(solution)/shard_map/pallas_call | solution.py:376
  59.1 1.8 %copy.13 = bf16[256,7168]{1,0:T(8,128)(2,1)} copy(bf16[256,7168]{1,0:T(8,128)(2,1)S(1)} %get-tuple-element.3) | data formatting | bytes 7340032
  60.9 0.7 %copy.15 = f32[2,16,2048]{2,1,0:T(8,128)} copy(f32[2,16,2048]{2,1,0:T(8,128)S(1)} %get-tuple-element.5) | data formatting | bytes 524288
  61.6 0.9 %copy.14 = f32[2,16,7168]{2,1,0:T(8,128)} copy(f32[2,16,7168]{2,1,0:T(8,128)S(1)} %get-tuple-element.4) | data formatting | bytes 1835008
Async XLA Ops:
  0.6 1.0 %copy-start = (bf16[2,16,7168]{2,1,0:T(8,128)(2,1)S(1)}, bf16[2,16,7168]{2,1,0:T(8,128)(2,1)}, u32[]{:S(2)}) copy-start(bf16[2,16,7168]{2,1,0:T(8,128)(2,1)} %adn.1) | copy-start | bytes 1376260
  1.7 0.9 %copy-start.1 = (bf16[2,16,2048]{2,1,0:T(8,128)(2,1)S(1)}, bf16[2,16,2048]{2,1,0:T(8,128)(2,1)}, u32[]{:S(2)}) copy-start(bf16[2,16,2048]{2,1,0:T(8,128)(2,1)} %aup.1) | copy-start | bytes 393220
  2.6 0.7 %copy-start.2 = (s32[16]{0:T(128)S(1)}, s32[16]{0:T(128)}, u32[]{:S(2)}) copy-start(s32[16]{0:T(128)} %counts.1) | copy-start | bytes 196
  3.2 0.7 %copy-start.3 = (s32[16]{0:T(128)S(1)}, s32[16]{0:T(128)}, u32[]{:S(2)}) copy-start(s32[16]{0:T(128)} %offsets.1) | copy-start | bytes 196
  3.9 0.7 %copy-start.4 = (s32[16]{0:T(128)S(1)}, s32[16]{0:T(128)}, u32[]{:S(2)}) copy-start(s32[16]{0:T(128)} %slots.1) | copy-start | bytes 196

commit v3 on v2

--- a/solution.py
+++ b/solution.py
@@ -20,9 +20,9 @@
 
 def kernel(
     dp_count, tensor_count, sends,
-    counts, offsets, slots, og_in, hid_in, adn, aup,
+    counts_in, offsets_in, slots_in, og_in, hid_in, adn, aup,
     out_h, out_d, out_u,
-    og, hid, gath_d, gath_u, z_up, z_dn,
+    counts, offsets, slots, og, hid, gath_d, gath_u, z_up, z_dn,
     sib_d, sib_u, got_d, got_u, sum_d, sum_u,
     one_d0, one_d1, one_u0, one_u1, two_d0, two_d1, two_u0, two_u1,
     load_sem, send_sem, gath_sem, z_sem, sib_sem, one_sem0, one_sem1, two_sem0, two_sem1,
@@ -67,6 +67,9 @@
         pltpu.make_async_copy(og_in, og, load_sem.at[1]),
         pltpu.make_async_copy(hid_in, hid, load_sem.at[2]),
         pltpu.make_async_copy(adn, gath_d.at[me], load_sem.at[3]),
+        pltpu.make_async_copy(counts_in, counts, load_sem.at[4]),
+        pltpu.make_async_copy(offsets_in, offsets, load_sem.at[5]),
+        pltpu.make_async_copy(slots_in, slots, load_sem.at[6]),
     ]
     for load in loads:
         load.start()
@@ -129,6 +132,8 @@
                 arrived(gath.at[origin, half], gath_sem.at[which, origin, half])
 
     gather_own(0, aup, gath_u)
+    for load in loads[4:]:
+        load.wait()
     position = me * tokens + lax.broadcasted_iota(jnp.int32, (1, tokens), 1)
     slot_of = jnp.zeros((1, tokens), jnp.int32)
     for adapter in range(counts.shape[0]):
@@ -137,23 +142,13 @@
         slot_of = slot_of + jnp.where(inside, slots[adapter], 0)
 
     def tile_of(width):
-        return math.gcd(width, 512)
+        return math.gcd(width, 1024)
 
     def partial_signal(values, gath):
-        width = values.shape[1]
-        tile = tile_of(width)
         rows = dp_count * per_owner * rank
-
-        def step(at, total):
-            cols = pl.ds(pl.multiple_of(at * tile, tile), tile)
-            maps = gath[:, :, :, cols].reshape(rows, tile)
-            return total + lax.dot_general(
-                maps, values[:, cols], (((1,), (1,)), ((), ())),
-                preferred_element_type=jnp.float32,
-            )
-
-        scores = lax.fori_loop(
-            0, width // tile, step, jnp.zeros((rows, tokens), jnp.float32)
+        scores = lax.dot_general(
+            gath[...].reshape(rows, values.shape[1]), values[...], (((1,), (1,)), ((), ())),
+            preferred_element_type=jnp.float32,
         ).reshape(dp_count * per_owner, rank, tokens)
         total = jnp.zeros((rank, tokens), jnp.float32)
         for slot in range(dp_count * per_owner):
@@ -194,13 +189,11 @@
         width = values.shape[1]
         tile = tile_of(width)
 
-        def step(at, _):
-            cols = pl.ds(pl.multiple_of(at * tile, tile), tile)
+        for at in range(width // tile):
+            cols = slice(at * tile, (at + 1) * tile)
             term = jnp.dot(rows, values[:, cols], preferred_element_type=jnp.float32)
             sib[:, :, :, cols] = term.astype(jnp.bfloat16).reshape(chips, per_owner, rank, tile)
-            return 0
-
-        lax.fori_loop(0, width // tile, step, 0)
+
         push(sib, got, sib_sem.at[which], dp=sibling)
 
     def sums_first(which, signal, values, got, total, one):
@@ -209,15 +202,13 @@
         tile = tile_of(width)
         arrived(got, sib_sem.at[which])
 
-        def step(at, _):
-            cols = pl.ds(pl.multiple_of(at * tile, tile), tile)
+        for at in range(width // tile):
+            cols = slice(at * tile, (at + 1) * tile)
             term = jnp.dot(rows, values[:, cols], preferred_element_type=jnp.float32)
             term = term.reshape(chips, per_owner, rank, tile)
             term = term + got[:, :, :, cols].astype(jnp.float32)
             total[:, :, :, cols] = term.astype(jnp.bfloat16)
-            return 0
-
-        lax.fori_loop(0, width // tile, step, 0)
+
         sems = (one_sem0, one_sem1)
         for far in (True, False):
             for half in range(per_owner):
@@ -285,10 +276,10 @@
     loads[0].wait()
     loads[1].wait()
     share(0, z_up, partial_signal(og, gath_u))
+    gather_first(1, gath_d)
     loads[2].wait()
     up_signal = shared(0, z_up)
     sums_sibling(0, up_signal, hid, sib_d, got_d)
-    gather_first(1, gath_d)
     sums_first(0, up_signal, hid, got_d, sum_d, one_d)
     gather_second(1, gath_d)
     gather_sibling(1, gath_d)
@@ -299,14 +290,11 @@
     tokens_by_row = spread(up_signal, range(dp_count * per_owner)).T.astype(jnp.bfloat16)
     tile = tile_of(hid.shape[1])
 
-    def hidden_step(at, _):
-        cols = pl.ds(pl.multiple_of(at * tile, tile), tile)
+    for at in range(hid.shape[1] // tile):
+        cols = slice(at * tile, (at + 1) * tile)
         maps = gath_d[:, :, :, cols].reshape(all_rows, tile)
         term = jnp.dot(tokens_by_row, maps, preferred_element_type=jnp.float32)
         out_h[:, cols] = (adapter_factor * term).astype(out_h.dtype)
-        return 0
-
-    lax.fori_loop(0, hid.shape[1] // tile, hidden_step, 0)
 
     down_signal = shared(1, z_dn)
     sums_sibling(1, down_signal, og, sib_u, got_u)
@@ -318,6 +306,17 @@
     for copy in started:
         copy.wait_send()
     assert len(started) == sends, (len(started), sends)
+
+
+def write_out(h, d, u, out_h, out_d, out_u, sem):
+    copies = [
+        pltpu.make_async_copy(src, dst, sem.at[at])
+        for at, (src, dst) in enumerate(((h, out_h), (d, out_d), (u, out_u)))
+    ]
+    for copy in copies:
+        copy.start()
+    for copy in copies:
+        copy.wait()
 
 
 def send_count(dp_count, tensor_count, per_owner):
@@ -343,8 +342,11 @@
     bf16, f32 = jnp.bfloat16, jnp.float32
     dma = pltpu.SemaphoreType.DMA
     vmem = pl.BlockSpec(memory_space=pltpu.VMEM)
-    smem = pl.BlockSpec(memory_space=pltpu.SMEM)
+    any_space = pl.BlockSpec(memory_space=pl.ANY)
     scratch = [
+        pltpu.SMEM(counts.shape, jnp.int32),
+        pltpu.SMEM(offsets.shape, jnp.int32),
+        pltpu.SMEM(adapter_slot.shape, jnp.int32),
         pltpu.VMEM((tokens, narrow), bf16),
         pltpu.VMEM((tokens, wide), bf16),
         pltpu.VMEM((dp_count, per_owner, rank, wide), bf16),
@@ -362,7 +364,7 @@
         scratch.append(pltpu.VMEM((size_b, rank, width), bf16))
         scratch.append(pltpu.VMEM((size_a, rank, width), bf16))
     scratch += [
-        dma((4,)),
+        dma((7,)),
         dma((sends,)),
         dma((2, dp_count, per_owner)),
         dma((2, tensor_count)),
@@ -373,14 +375,14 @@
         dma((2, size_a)),
     ]
     rows = dp_count * per_owner * rank
-    return pl.pallas_call(
+    results = pl.pallas_call(
         functools.partial(kernel, dp_count, tensor_count, sends),
         out_shape=(
             pltpu.VMEM((tokens, wide), bf16),
             pltpu.VMEM((per_owner, rank, wide), f32),
             pltpu.VMEM((per_owner, rank, narrow), f32),
         ),
-        in_specs=[smem] * 3 + [pl.BlockSpec(memory_space=pl.ANY)] * 4,
+        in_specs=[any_space] * 7,
         out_specs=(vmem, vmem, vmem),
         scratch_shapes=scratch,
         compiler_params=pltpu.CompilerParams(
@@ -391,7 +393,22 @@
             bytes_accessed=2 * tokens * (2 * wide + narrow),
             transcendentals=0,
         ),
-    )(counts, offsets, adapter_slot, output_gradient, hidden, adapter_down, adapter_up)
+    )(*(
+        pltpu.with_memory_space_constraint(array, pltpu.HBM)
+        for array in (
+            counts, offsets, adapter_slot, output_gradient, hidden, adapter_down, adapter_up
+        )
+    ))
+    return pl.pallas_call(
+        write_out,
+        out_shape=tuple(jax.ShapeDtypeStruct(r.shape, r.dtype) for r in results),
+        in_specs=[any_space] * 3,
+        out_specs=(any_space,) * 3,
+        scratch_shapes=[dma((3,))],
+        cost_estimate=pl.CostEstimate(
+            flops=0, bytes_accessed=2 * tokens * wide, transcendentals=0
+        ),
+    )(*results)
 
 
 def solution(mesh):

time: 62.7 us -> 199 us (3.17)
  Pallas kernels: 54.5 us -> 195 us
  local copies, waits for them, and re-layouts: 7.34 us -> 3.39 us
    pallas_call x0 -> x1, Pallas kernels: none -> 148 us  [on_device(): pl.pallas_call(write_out, out_shape=tuple((jax.ShapeDtypeStruct(r.shape,...]
    pallas_call x1, Pallas kernels: 54.5 us -> 46.8 us  [on_device(): pl.pallas_call(functools.partial(kernel, dp_count, tensor_count, sends),...]
    unnamed x13 -> x6, local copies, waits for them, and re-layouts: 7.34 us -> 3.39 us
where the time goes in v3:
time: 199 us
  Pallas kernels  195 us (98%)
  local copies, waits for them, and re-layouts  3.39 us (2%)
    pallas_call x1, Pallas kernels, on_device(): pl.pallas_call(write_out, out_shape=tuple((jax.ShapeDtypeStruct(r.shape,...  148 us
    pallas_call x1, Pallas kernels, on_device(): pl.pallas_call(functools.partial(kernel, dp_count, tensor_count, sends),...  46.8 us

profile of v3, /device:TPU:0, one launch (start us, length us, event | category | flops | bytes accessed | tf_op | source)
XLA Modules:
  0.0 198.9 jit_solution(193299937218826993)
XLA Ops:
  0.6 46.8 %shard_map.94 = (bf16[256,7168]{1,0:T(8,128)(2,1)S(1)}, f32[2,16,7168]{2,1,0:T(8,128)S(1)}, f32[2,16,2048]{2,1,0:T(8,128)S(1)}) custom-call(s32[16]{0:T(128)} %counts_in.1, s32[16]{0:T(128)} %offsets_in.1, s32[16]{0:T(128)} %slots_in.1, bf16[256,2048]{1,0:T(8,128)(2,1)} %og_in.1, bf16[256,7168]{1,0:T(8,128)(2,1)} %hid_in.1, bf16[2,16,7168]{2,1,0:T(8,128)(2,1)} %adn.1, ...), custom_call_target="tpu_custom_call" | custom-call | flops 3355443200 | bytes 8388608 | tf_op jit(solution)/shard_map/pallas_call | solution.py:378
  47.4 0.0 copy-start
  47.4 1.8 copy-done
  49.2 0.0 copy-start.1
  49.2 0.9 copy-done.1
  50.1 0.0 copy-start.2
  50.1 0.7 copy-done.2
  50.8 148.0 %shard_map.95 = (bf16[256,7168]{1,0:T(8,128)(2,1)}, f32[2,16,7168]{2,1,0:T(8,128)}, f32[2,16,2048]{2,1,0:T(8,128)}) custom-call(bf16[256,7168]{1,0:T(8,128)(2,1)} %copy-done, f32[2,16,7168]{2,1,0:T(8,128)} %copy-done.1, f32[2,16,2048]{2,1,0:T(8,128)} %copy-done.2), custom_call_target="tpu_custom_call" | custom-call | bytes 3670016 | tf_op jit(solution)/shard_map/pallas_call | solution.py:402
Async XLA Ops:
  47.4 1.8 copy-start
  49.2 0.9 copy-start.1
  50.1 0.7 copy-start.2

commit v4 on v3

--- a/solution.py
+++ b/solution.py
@@ -19,7 +19,7 @@
 
 
 def kernel(
-    dp_count, tensor_count, sends,
+    dp_count, tensor_count, sends, pieces,
     counts_in, offsets_in, slots_in, og_in, hid_in, adn, aup,
     out_h, out_d, out_u,
     counts, offsets, slots, og, hid, gath_d, gath_u, z_up, z_dn,
@@ -112,18 +112,17 @@
                     push(block, block, recv, dp=to)
                 push(block, block, recv, dp=sibling)
 
-    def gather_second(which, gath):
-        for near in (True, False):
-            for half in range(per_owner):
-                first, n_first, second, n_second = axes(half)
-                for off2 in range(1, n_second):
-                    for off in range(0, 1) if near else range(1, n_first):
-                        origin = chip_of(
-                            half, (first + off) % n_first, (second + off2) % n_second
-                        ) * 2 + core
-                        block, recv = gath.at[origin, half], gath_sem.at[which, origin, half]
-                        arrived(block, recv)
-                        push(block, block, recv, dp=sibling)
+    def gather_second(which, gath, near):
+        for half in range(per_owner):
+            first, n_first, second, n_second = axes(half)
+            for off2 in range(1, n_second):
+                for off in range(0, 1) if near else range(1, n_first):
+                    origin = chip_of(
+                        half, (first + off) % n_first, (second + off2) % n_second
+                    ) * 2 + core
+                    block, recv = gath.at[origin, half], gath_sem.at[which, origin, half]
+                    arrived(block, recv)
+                    push(block, block, recv, dp=sibling)
 
     def gather_sibling(which, gath):
         for other in range(chips):
@@ -184,31 +183,36 @@
             for half in range(per_owner)
         ]
 
-    def sums_sibling(which, signal, values, sib, got):
-        rows = spread(signal, numbers_of(1 - core)).astype(jnp.bfloat16)
-        width = values.shape[1]
-        tile = tile_of(width)
-
-        for at in range(width // tile):
-            cols = slice(at * tile, (at + 1) * tile)
+    def piece_of(which, piece, width):
+        return pl.ds(piece * (width // pieces[which]), width // pieces[which])
+
+    def gradient_rows(which_core, signal):
+        return spread(signal, numbers_of(which_core)).astype(jnp.bfloat16)
+
+    def tiles(which, piece, width):
+        size = width // pieces[which]
+        tile = math.gcd(size, 1024)
+        return [pl.ds(piece * size + at, tile) for at in range(0, size, tile)]
+
+    def sums_sibling(which, piece, rows, values, sib, got):
+        for cols in tiles(which, piece, values.shape[1]):
             term = jnp.dot(rows, values[:, cols], preferred_element_type=jnp.float32)
-            sib[:, :, :, cols] = term.astype(jnp.bfloat16).reshape(chips, per_owner, rank, tile)
-
-        push(sib, got, sib_sem.at[which], dp=sibling)
-
-    def sums_first(which, signal, values, got, total, one):
-        rows = spread(signal, numbers_of(core)).astype(jnp.bfloat16)
-        width = values.shape[1]
-        tile = tile_of(width)
-        arrived(got, sib_sem.at[which])
-
-        for at in range(width // tile):
-            cols = slice(at * tile, (at + 1) * tile)
+            sib[:, :, :, cols] = term.astype(jnp.bfloat16).reshape(
+                chips, per_owner, rank, cols.size
+            )
+        part = piece_of(which, piece, values.shape[1])
+        push(
+            sib.at[:, :, :, part], got.at[:, :, :, part], sib_sem.at[which, piece], dp=sibling
+        )
+
+    def sums_first(which, piece, rows, values, got, total, one):
+        part = piece_of(which, piece, values.shape[1])
+        arrived(got.at[:, :, :, part], sib_sem.at[which, piece])
+        for cols in tiles(which, piece, values.shape[1]):
             term = jnp.dot(rows, values[:, cols], preferred_element_type=jnp.float32)
-            term = term.reshape(chips, per_owner, rank, tile)
+            term = term.reshape(chips, per_owner, rank, cols.size)
             term = term + got[:, :, :, cols].astype(jnp.float32)
             total[:, :, :, cols] = term.astype(jnp.bfloat16)
-
         sems = (one_sem0, one_sem1)
         for far in (True, False):
             for half in range(per_owner):
@@ -219,59 +223,65 @@
                     for off2 in range(1, n_second) if far else range(0, 1):
                         owner_second = (second + off2) % n_second
                         push(
-                            total.at[chip_of(half, peer, owner_second), half],
-                            one[half].at[first, owner_second],
-                            sems[half].at[which, first, owner_second],
+                            total.at[chip_of(half, peer, owner_second), half, :, part],
+                            one[half].at[first, owner_second, :, part],
+                            sems[half].at[which, piece, first, owner_second],
                             dp=to,
                         )
 
-    def sums_second(which, total, one, two):
+    def sums_second(which, piece, total, one, two):
+        part = piece_of(which, piece, total.shape[3])
         sems, sems2 = (one_sem0, one_sem1), (two_sem0, two_sem1)
         for half in range(per_owner):
             first, n_first, second, n_second = axes(half)
             for off2 in range(1, n_second):
                 owner_second = (second + off2) % n_second
                 owner = chip_of(half, first, owner_second)
-                value = total[owner, half].astype(jnp.float32)
+                value = total[owner, half, :, part].astype(jnp.float32)
                 for off in range(1, n_first):
                     peer = (first + off) % n_first
                     arrived(
-                        one[half].at[peer, owner_second],
-                        sems[half].at[which, peer, owner_second],
+                        one[half].at[peer, owner_second, :, part],
+                        sems[half].at[which, piece, peer, owner_second],
                     )
-                    value = value + one[half][peer, owner_second].astype(jnp.float32)
-                total[pl.ds(owner, 1), half] = value.astype(jnp.bfloat16)[None]
+                    value = value + one[half][peer, owner_second, :, part].astype(jnp.float32)
+                total[pl.ds(owner, 1), half, :, part] = value.astype(jnp.bfloat16)[None]
                 push(
-                    total.at[owner, half], two[half].at[second],
-                    sems2[half].at[which, second], dp=owner * 2 + core,
+                    total.at[owner, half, :, part], two[half].at[second, :, part],
+                    sems2[half].at[which, piece, second], dp=owner * 2 + core,
                 )
 
-    def sums_last(which, total, one, two, out):
+    def sums_last(which, piece, total, one, two, out):
+        part = piece_of(which, piece, total.shape[3])
         sems, sems2 = (one_sem0, one_sem1), (two_sem0, two_sem1)
         for half in range(per_owner):
             first, n_first, second, n_second = axes(half)
-            value = total[chip, half].astype(jnp.float32)
+            value = total[chip, half, :, part].astype(jnp.float32)
             for off in range(1, n_first):
                 peer = (first + off) % n_first
-                arrived(one[half].at[peer, second], sems[half].at[which, peer, second])
-                value = value + one[half][peer, second].astype(jnp.float32)
+                arrived(
+                    one[half].at[peer, second, :, part],
+                    sems[half].at[which, piece, peer, second],
+                )
+                value = value + one[half][peer, second, :, part].astype(jnp.float32)
             for off2 in range(1, n_second):
                 peer = (second + off2) % n_second
-                arrived(two[half].at[peer], sems2[half].at[which, peer])
-                value = value + two[half][peer].astype(jnp.float32)
+                arrived(two[half].at[peer, :, part], sems2[half].at[which, piece, peer])
+                value = value + two[half][peer, :, part].astype(jnp.float32)
             number = me * per_owner + half
             held = jnp.zeros((1, 1), jnp.int32)
             for adapter in range(counts.shape[0]):
                 mine = jnp.full((1, 1), slots[adapter], jnp.int32) == number
                 held = held + jnp.where(mine, counts[adapter], 0)
-            out[half] = value * (adapter_factor / held.astype(jnp.float32))
+            out[half, :, part] = value * (adapter_factor / held.astype(jnp.float32))
 
     one_d, one_u = (one_d0, one_d1), (one_u0, one_u1)
     two_d, two_u = (two_d0, two_d1), (two_u0, two_u1)
 
     gather_first(0, gath_u)
     gather_own(1, adn, gath_d)
-    gather_second(0, gath_u)
+    gather_second(0, gath_u, True)
+    gather_second(0, gath_u, False)
     gather_sibling(0, gath_u)
     loads[0].wait()
     loads[1].wait()
@@ -279,9 +289,15 @@
     gather_first(1, gath_d)
     loads[2].wait()
     up_signal = shared(0, z_up)
-    sums_sibling(0, up_signal, hid, sib_d, got_d)
-    sums_first(0, up_signal, hid, got_d, sum_d, one_d)
-    gather_second(1, gath_d)
+    rows = gradient_rows(1 - core, up_signal)
+    for piece in range(pieces[0]):
+        sums_sibling(0, piece, rows, hid, sib_d, got_d)
+    rows = gradient_rows(core, up_signal)
+    sums_first(0, 0, rows, hid, got_d, sum_d, one_d)
+    gather_second(1, gath_d, True)
+    for piece in range(1, pieces[0]):
+        sums_first(0, piece, rows, hid, got_d, sum_d, one_d)
+    gather_second(1, gath_d, False)
     gather_sibling(1, gath_d)
     loads[3].wait()
     share(1, z_dn, partial_signal(hid, gath_d))
@@ -297,37 +313,35 @@
         out_h[:, cols] = (adapter_factor * term).astype(out_h.dtype)
 
     down_signal = shared(1, z_dn)
-    sums_sibling(1, down_signal, og, sib_u, got_u)
-    sums_first(1, down_signal, og, got_u, sum_u, one_u)
-    sums_second(0, sum_d, one_d, two_d)
-    sums_second(1, sum_u, one_u, two_u)
-    sums_last(0, sum_d, one_d, two_d, out_d)
-    sums_last(1, sum_u, one_u, two_u, out_u)
+    rows = gradient_rows(1 - core, down_signal)
+    for piece in range(pieces[1]):
+        sums_sibling(1, piece, rows, og, sib_u, got_u)
+    sums_second(0, 0, sum_d, one_d, two_d)
+    rows = gradient_rows(core, down_signal)
+    for piece in range(pieces[1]):
+        sums_first(1, piece, rows, og, got_u, sum_u, one_u)
+    for piece in range(1, pieces[0]):
+        sums_second(0, piece, sum_d, one_d, two_d)
+    for piece in range(pieces[1]):
+        sums_second(1, piece, sum_u, one_u, two_u)
+    for piece in range(pieces[0]):
+        sums_last(0, piece, sum_d, one_d, two_d, out_d)
+    for piece in range(pieces[1]):
+        sums_last(1, piece, sum_u, one_u, two_u, out_u)
     for copy in started:
         copy.wait_send()
     assert len(started) == sends, (len(started), sends)
 
 
-def write_out(h, d, u, out_h, out_d, out_u, sem):
-    copies = [
-        pltpu.make_async_copy(src, dst, sem.at[at])
-        for at, (src, dst) in enumerate(((h, out_h), (d, out_d), (u, out_u)))
-    ]
-    for copy in copies:
-        copy.start()
-    for copy in copies:
-        copy.wait()
-
-
-def send_count(dp_count, tensor_count, per_owner):
+def send_count(dp_count, tensor_count, per_owner, pieces):
     size_a, size_b = chip_grid(dp_count)
-    total = 2 * (tensor_count - 1) + 2
+    total = 2 * (tensor_count - 1) + sum(pieces)
     for half in range(per_owner):
         n_first, n_second = (size_a, size_b) if half == 0 else (size_b, size_a)
         own = n_first + n_second - 1
         relayed = (n_first - 1) * n_second + (n_second - 1) * n_first
         back = (n_first - 1) * n_second + (n_second - 1)
-        total += 2 * (own + relayed + back)
+        total += 2 * (own + relayed) + sum(pieces) * back
     return total
 
 
@@ -338,7 +352,8 @@
     per_owner, rank, wide = adapter_down.shape
     narrow = adapter_up.shape[2]
     tokens = hidden.shape[0]
-    sends = send_count(dp_count, tensor_count, per_owner)
+    pieces = (2, 1)
+    sends = send_count(dp_count, tensor_count, per_owner, pieces)
     bf16, f32 = jnp.bfloat16, jnp.float32
     dma = pltpu.SemaphoreType.DMA
     vmem = pl.BlockSpec(memory_space=pltpu.VMEM)
@@ -368,15 +383,15 @@
         dma((sends,)),
         dma((2, dp_count, per_owner)),
         dma((2, tensor_count)),
-        dma((2,)),
-        dma((2, size_a, size_b)),
-        dma((2, size_b, size_a)),
-        dma((2, size_b)),
-        dma((2, size_a)),
+        dma((2, max(pieces))),
+        dma((2, max(pieces), size_a, size_b)),
+        dma((2, max(pieces), size_b, size_a)),
+        dma((2, max(pieces), size_b)),
+        dma((2, max(pieces), size_a)),
     ]
     rows = dp_count * per_owner * rank
-    results = pl.pallas_call(
-        functools.partial(kernel, dp_count, tensor_count, sends),
+    return pl.pallas_call(
+        functools.partial(kernel, dp_count, tensor_count, sends, pieces),
         out_shape=(
             pltpu.VMEM((tokens, wide), bf16),
             pltpu.VMEM((per_owner, rank, wide), f32),
@@ -399,16 +414,6 @@
             counts, offsets, adapter_slot, output_gradient, hidden, adapter_down, adapter_up
         )
     ))
-    return pl.pallas_call(
-        write_out,
-        out_shape=tuple(jax.ShapeDtypeStruct(r.shape, r.dtype) for r in results),
-        in_specs=[any_space] * 3,
-        out_specs=(any_space,) * 3,
-        scratch_shapes=[dma((3,))],
-        cost_estimate=pl.CostEstimate(
-            flops=0, bytes_accessed=2 * tokens * wide, transcendentals=0
-        ),
-    )(*results)
 
 
 def solution(mesh):

time: 199 us -> 51.3 us (0.26)
  Pallas kernels: 195 us -> 47.1 us
    pallas_call x2 -> x1, Pallas kernels: 195 us -> 47.1 us  [on_device(): pl.pallas_call(functools.partial(kernel, dp_count, tensor_count, sends, p...]
where the time goes in v4:
time: 51.3 us; the launch traced here: 51.2 us
  Pallas kernels  47.1 us (92%)
  local copies, waits for them, and re-layouts  3.46 us (7%)
  between operations  0.64 us (1%)
    pallas_call x1, Pallas kernels, on_device(): pl.pallas_call(functools.partial(kernel, dp_count, tensor_count, sends, p...  47.1 us
    unnamed x3, local copies, waits for them, and re-layouts  3.46 us

profile of v4, /device:TPU:0, one launch (start us, length us, event | category | flops | bytes accessed | tf_op | source)
XLA Modules:
  0.0 51.2 jit_solution(4025364799418708566)
XLA Ops:
  0.6 47.1 %shard_map.94 = (bf16[256,7168]{1,0:T(8,128)(2,1)S(1)}, f32[2,16,7168]{2,1,0:T(8,128)S(1)}, f32[2,16,2048]{2,1,0:T(8,128)S(1)}) custom-call(s32[16]{0:T(128)} %counts_in.1, s32[16]{0:T(128)} %offsets_in.1, s32[16]{0:T(128)} %slots_in.1, bf16[256,2048]{1,0:T(8,128)(2,1)} %og_in.1, bf16[256,7168]{1,0:T(8,128)(2,1)} %hid_in.1, bf16[2,16,7168]{2,1,0:T(8,128)(2,1)} %adn.1, ...), custom_call_target="tpu_custom_call" | custom-call | flops 3355443200 | bytes 8388608 | tf_op jit(solution)/shard_map/pallas_call | solution.py:393
  47.7 1.8 %copy.13 = bf16[256,7168]{1,0:T(8,128)(2,1)} copy(bf16[256,7168]{1,0:T(8,128)(2,1)S(1)} %get-tuple-element.3) | data formatting | bytes 7340032
  49.6 0.7 %copy.15 = f32[2,16,2048]{2,1,0:T(8,128)} copy(f32[2,16,2048]{2,1,0:T(8,128)S(1)} %get-tuple-element.5) | data formatting | bytes 524288
  50.3 0.9 %copy.14 = f32[2,16,7168]{2,1,0:T(8,128)} copy(f32[2,16,7168]{2,1,0:T(8,128)S(1)} %get-tuple-element.4) | data formatting | bytes 1835008

commit v5 on v4

--- a/solution.py
+++ b/solution.py
@@ -86,17 +86,19 @@
         pl.semaphore_signal(barrier, inc=1, device_id=partner, device_id_type=MESH)
     pl.semaphore_wait(barrier, len(partners))
 
-    def gather_own(which, own, gath):
-        for along_first in (True, False):
-            for half in range(per_owner):
-                first, n_first, second, n_second = axes(half)
-                recv = gath_sem.at[which, me, half]
-                for off in range(1, n_first if along_first else n_second):
-                    if along_first:
-                        to = chip_of(half, (first + off) % n_first, second) * 2 + core
-                    else:
-                        to = chip_of(half, first, (second + off) % n_second) * 2 + core
-                    push(own.at[half], gath.at[me, half], recv, dp=to)
+    def gather_own(which, own, gath, along_first):
+        for half in range(per_owner):
+            first, n_first, second, n_second = axes(half)
+            for off in range(1, n_first if along_first else n_second):
+                if along_first:
+                    to = chip_of(half, (first + off) % n_first, second) * 2 + core
+                else:
+                    to = chip_of(half, first, (second + off) % n_second) * 2 + core
+                push(
+                    own.at[half], gath.at[me, half], gath_sem.at[which, me, half], dp=to
+                )
+
+    def gather_near(which, own, gath):
         for half in range(per_owner):
             push(own.at[half], gath.at[me, half], gath_sem.at[which, me, half], dp=sibling)
 
@@ -130,7 +132,10 @@
                 origin = other * 2 + (1 - core)
                 arrived(gath.at[origin, half], gath_sem.at[which, origin, half])
 
-    gather_own(0, aup, gath_u)
+    gather_own(0, aup, gath_u, True)
+    gather_own(0, aup, gath_u, False)
+    gather_near(0, aup, gath_u)
+    gather_own(1, adn, gath_d, True)
     for load in loads[4:]:
         load.wait()
     position = me * tokens + lax.broadcasted_iota(jnp.int32, (1, tokens), 1)
@@ -279,7 +284,8 @@
     two_d, two_u = (two_d0, two_d1), (two_u0, two_u1)
 
     gather_first(0, gath_u)
-    gather_own(1, adn, gath_d)
+    gather_own(1, adn, gath_d, False)
+    gather_near(1, adn, gath_d)
     gather_second(0, gath_u, True)
     gather_second(0, gath_u, False)
     gather_sibling(0, gath_u)

time: 51.3 us -> 51.3 us (level)
  no operation moved by 1% of the time
where the time goes in v5:
time: 51.3 us; the launch traced here: 51.1 us
  Pallas kernels  47 us (92%)
  local copies, waits for them, and re-layouts  3.46 us (7%)
  between operations  0.64 us (1%)
    pallas_call x1, Pallas kernels, on_device(): pl.pallas_call(functools.partial(kernel, dp_count, tensor_count, sends, p...  47 us
    unnamed x3, local copies, waits for them, and re-layouts  3.46 us

profile of v5, /device:TPU:0, one launch (start us, length us, event | category | flops | bytes accessed | tf_op | source)
XLA Modules:
  0.0 51.1 jit_solution(16629501010785732387)
XLA Ops:
  0.6 47.0 %shard_map.94 = (bf16[256,7168]{1,0:T(8,128)(2,1)S(1)}, f32[2,16,7168]{2,1,0:T(8,128)S(1)}, f32[2,16,2048]{2,1,0:T(8,128)S(1)}) custom-call(s32[16]{0:T(128)} %counts_in.1, s32[16]{0:T(128)} %offsets_in.1, s32[16]{0:T(128)} %slots_in.1, bf16[256,2048]{1,0:T(8,128)(2,1)} %og_in.1, bf16[256,7168]{1,0:T(8,128)(2,1)} %hid_in.1, bf16[2,16,7168]{2,1,0:T(8,128)(2,1)} %adn.1, ...), custom_call_target="tpu_custom_call" | custom-call | flops 3355443200 | bytes 8388608 | tf_op jit(solution)/shard_map/pallas_call | solution.py:399
  47.7 1.8 %copy.13 = bf16[256,7168]{1,0:T(8,128)(2,1)} copy(bf16[256,7168]{1,0:T(8,128)(2,1)S(1)} %get-tuple-element.3) | data formatting | bytes 7340032
  49.5 0.7 %copy.15 = f32[2,16,2048]{2,1,0:T(8,128)} copy(f32[2,16,2048]{2,1,0:T(8,128)S(1)} %get-tuple-element.5) | data formatting | bytes 524288
  50.2 0.9 %copy.14 = f32[2,16,7168]{2,1,0:T(8,128)} copy(f32[2,16,7168]{2,1,0:T(8,128)S(1)} %get-tuple-element.4) | data formatting | bytes 1835008

commit v6 on v4

--- a/solution.py
+++ b/solution.py
@@ -331,6 +331,17 @@
     for copy in started:
         copy.wait_send()
     assert len(started) == sends, (len(started), sends)
+
+
+def write_out(h, d, u, out_h, out_d, out_u, sem):
+    copies = [
+        pltpu.make_async_copy(src, dst, sem.at[at])
+        for at, (src, dst) in enumerate(((h, out_h), (d, out_d), (u, out_u)))
+    ]
+    for copy in copies:
+        copy.start()
+    for copy in copies:
+        copy.wait()
 
 
 def send_count(dp_count, tensor_count, per_owner, pieces):
@@ -390,7 +401,7 @@
         dma((2, max(pieces), size_a)),
     ]
     rows = dp_count * per_owner * rank
-    return pl.pallas_call(
+    results = pl.pallas_call(
         functools.partial(kernel, dp_count, tensor_count, sends, pieces),
         out_shape=(
             pltpu.VMEM((tokens, wide), bf16),
@@ -414,6 +425,17 @@
             counts, offsets, adapter_slot, output_gradient, hidden, adapter_down, adapter_up
         )
     ))
+    return pl.pallas_call(
+        write_out,
+        out_shape=tuple(pltpu.HBM(r.shape, r.dtype) for r in results),
+        in_specs=[any_space] * 3,
+        out_specs=(any_space,) * 3,
+        scratch_shapes=[dma((3,))],
+        compiler_params=pltpu.CompilerParams(vmem_limit_bytes=2 * 2**20),
+        cost_estimate=pl.CostEstimate(
+            flops=0, bytes_accessed=2 * tokens * wide, transcendentals=0
+        ),
+    )(*(pltpu.with_memory_space_constraint(r, pltpu.VMEM) for r in results))
 
 
 def solution(mesh):

time: 51.3 us -> 50.1 us (0.977)
  local copies, waits for them, and re-layouts: 3.46 us -> 0 us
  Pallas kernels: 47.1 us -> 49.3 us
    unnamed x3 -> x0, local copies, waits for them, and re-layouts: 3.46 us -> none
    pallas_call x0 -> x1, Pallas kernels: none -> 2.24 us  [on_device(): pl.pallas_call(write_out, out_shape=tuple((pltpu.HBM(r.shape, r.dtype) fo...]
where the time goes in v6:
time: 50.1 us; the launch traced here: 50 us
  Pallas kernels  49.3 us (98%)
  between operations  0.64 us (1%)
    pallas_call x1, Pallas kernels, on_device(): pl.pallas_call(functools.partial(kernel, dp_count, tensor_count, sends, p...  47.1 us
    pallas_call x1, Pallas kernels, on_device(): pl.pallas_call(write_out, out_shape=tuple((pltpu.HBM(r.shape, r.dtype) fo...  2.24 us

profile of v6, /device:TPU:0, one launch (start us, length us, event | category | flops | bytes accessed | tf_op | source)
XLA Modules:
  0.0 50.0 jit_solution(6541257054237674211)
XLA Ops:
  0.6 47.1 %shard_map.94 = (bf16[256,7168]{1,0:T(8,128)(2,1)S(1)}, f32[2,16,7168]{2,1,0:T(8,128)S(1)}, f32[2,16,2048]{2,1,0:T(8,128)S(1)}) custom-call(s32[16]{0:T(128)} %counts_in.1, s32[16]{0:T(128)} %offsets_in.1, s32[16]{0:T(128)} %slots_in.1, bf16[256,2048]{1,0:T(8,128)(2,1)} %og_in.1, bf16[256,7168]{1,0:T(8,128)(2,1)} %hid_in.1, bf16[2,16,7168]{2,1,0:T(8,128)(2,1)} %adn.1, ...), custom_call_target="tpu_custom_call" | custom-call | flops 3355443200 | bytes 8388608 | tf_op jit(solution)/shard_map/pallas_call | solution.py:404
  47.7 2.2 %shard_map.95 = (bf16[256,7168]{1,0:T(8,128)(2,1)}, f32[2,16,7168]{2,1,0:T(8,128)}, f32[2,16,2048]{2,1,0:T(8,128)}) custom-call(bf16[256,7168]{1,0:T(8,128)(2,1)S(1)} %get-tuple-element.6.h, f32[2,16,7168]{2,1,0:T(8,128)S(1)} %get-tuple-element.7.d, f32[2,16,2048]{2,1,0:T(8,128)S(1)} %get-tuple-element.8.u), custom_call_target="tpu_custom_call" | custom-call | bytes 3670016 | tf_op jit(solution)/shard_map/pallas_call | solution.py:428

commit v7 on v6

--- a/solution.py
+++ b/solution.py
@@ -305,17 +305,21 @@
     all_rows = dp_count * per_owner * rank
     tokens_by_row = spread(up_signal, range(dp_count * per_owner)).T.astype(jnp.bfloat16)
     tile = tile_of(hid.shape[1])
-
-    for at in range(hid.shape[1] // tile):
-        cols = slice(at * tile, (at + 1) * tile)
-        maps = gath_d[:, :, :, cols].reshape(all_rows, tile)
-        term = jnp.dot(tokens_by_row, maps, preferred_element_type=jnp.float32)
-        out_h[:, cols] = (adapter_factor * term).astype(out_h.dtype)
-
+    steps = hid.shape[1] // tile
+
+    def hidden_tiles(begin, end):
+        for at in range(begin, end):
+            cols = slice(at * tile, (at + 1) * tile)
+            maps = gath_d[:, :, :, cols].reshape(all_rows, tile)
+            term = jnp.dot(tokens_by_row, maps, preferred_element_type=jnp.float32)
+            out_h[:, cols] = (adapter_factor * term).astype(out_h.dtype)
+
+    hidden_tiles(0, steps // 2)
     down_signal = shared(1, z_dn)
     rows = gradient_rows(1 - core, down_signal)
     for piece in range(pieces[1]):
         sums_sibling(1, piece, rows, og, sib_u, got_u)
+    hidden_tiles(steps // 2, steps)
     sums_second(0, 0, sum_d, one_d, two_d)
     rows = gradient_rows(core, down_signal)
     for piece in range(pieces[1]):

time: 50.1 us -> 50.8 us (1.014)
  Pallas kernels: 49.3 us -> 50 us
    pallas_call x1, Pallas kernels: 47.1 us -> 47.8 us  [on_device(): pl.pallas_call(functools.partial(kernel, dp_count, tensor_count, sends, p...]
where the time goes in v7:
time: 50.8 us; the launch traced here: 50.7 us
  Pallas kernels  50 us (98%)
  between operations  0.64 us (1%)
    pallas_call x1, Pallas kernels, on_device(): pl.pallas_call(functools.partial(kernel, dp_count, tensor_count, sends, p...  47.8 us
    pallas_call x1, Pallas kernels, on_device(): pl.pallas_call(write_out, out_shape=tuple((pltpu.HBM(r.shape, r.dtype) fo...  2.24 us

profile of v7, /device:TPU:0, one launch (start us, length us, event | category | flops | bytes accessed | tf_op | source)
XLA Modules:
  0.0 50.7 jit_solution(17836574950966241900)
XLA Ops:
  0.6 47.8 %shard_map.94 = (bf16[256,7168]{1,0:T(8,128)(2,1)S(1)}, f32[2,16,7168]{2,1,0:T(8,128)S(1)}, f32[2,16,2048]{2,1,0:T(8,128)S(1)}) custom-call(s32[16]{0:T(128)} %counts_in.1, s32[16]{0:T(128)} %offsets_in.1, s32[16]{0:T(128)} %slots_in.1, bf16[256,2048]{1,0:T(8,128)(2,1)} %og_in.1, bf16[256,7168]{1,0:T(8,128)(2,1)} %hid_in.1, bf16[2,16,7168]{2,1,0:T(8,128)(2,1)} %adn.1, ...), custom_call_target="tpu_custom_call" | custom-call | flops 3355443200 | bytes 8388608 | tf_op jit(solution)/shard_map/pallas_call | solution.py:408
  48.4 2.2 %shard_map.95 = (bf16[256,7168]{1,0:T(8,128)(2,1)}, f32[2,16,7168]{2,1,0:T(8,128)}, f32[2,16,2048]{2,1,0:T(8,128)}) custom-call(bf16[256,7168]{1,0:T(8,128)(2,1)S(1)} %get-tuple-element.6.h, f32[2,16,7168]{2,1,0:T(8,128)S(1)} %get-tuple-element.7.d, f32[2,16,2048]{2,1,0:T(8,128)S(1)} %get-tuple-element.8.u), custom_call_target="tpu_custom_call" | custom-call | bytes 3670016 | tf_op jit(solution)/shard_map/pallas_call | solution.py:432
